TPU v7x, 512 devices: a whole 4x4x16 slice. The times are simulated.
512 devices in a mesh: dp: 64 (over y, z_lo, core), blk: 8 (over z_hi, x).
Axes of the slice: x: 4, y: 4, z: 16 (z_hi: 2, z_lo: 8; z = z_hi * 8 + z_lo), core: 2. Of those that a mesh axis runs over, the one named last changes fastest.
Arguments:
- images: float32 [65536, 1152], P(('dp', 'blk')), may hold values from -12 to 12
- texts: float32 [65536, 1152], P(('dp', 'blk')), may hold values from -6 to 6
- positives: int32 [65536], P(('dp', 'blk')), may hold values from 0 to 127, as said below
- plan: int32 [3, 64], replicated, may hold values from 0 to 63, as said below
Outputs:
- image_grad: float32 [65536, 1152], P(('dp', 'blk'))
- text_grad: float32 [65536, 1152], P(('dp', 'blk'))
- totals: float32 [3], replicated
Inputs may be any that keep to these rules, and one draw needn't show every extreme that they name: Within each device's block of 128 rows, positives holds every number 0 to 127 once. Each row of plan pairs the indices of dp: plan[r, plan[r, a]] = a and plan[r, a] != a. No two rounds pair the same two indices.
All inputs are finite; a program needn't handle non-finite values.
Results may differ from a plain program's by a relative error of at most 0.005.
Values may be sent and summed in bfloat16 or wider, within the bound.
A program may use at most 64 MiB of HBM per device.

v0:
```python
import math
import jax
import jax.numpy as jnp
from jax import lax
from jax.sharding import PartitionSpec as P

LOGIT_SHARPNESS = 2.0
LOGIT_OFFSET = -2.0


def similarity(left, right, scale_factor):
    return (
        lax.dot_general(left, right, (((1,), (1,)), ((), ())), preferred_element_type=jnp.float32)
        * scale_factor
    )


def pair_terms(similarity_matrix, target_signs):
    pair_logits = LOGIT_SHARPNESS * similarity_matrix + LOGIT_OFFSET
    weights = jax.nn.sigmoid(pair_logits) - target_signs
    losses = jax.nn.softplus(pair_logits) - target_signs * pair_logits
    stats = jnp.stack([jnp.sum(losses), jnp.sum(weights), jnp.sum(weights * similarity_matrix)])
    return (weights.astype(jnp.bfloat16), stats)


def row_sum(weights, other):
    return jnp.dot(weights, other, preferred_element_type=jnp.float32)


def column_sum(weights, other):
    return lax.dot_general(
        weights, other, (((0,), (0,)), ((), ())), preferred_element_type=jnp.float32
    )


def body(images, texts, positives, plan):
    rows, width = images.shape
    peers = lax.axis_size("dp")
    share = rows // peers
    rounds = plan.shape[0]
    scale_factor = 1.0 / math.sqrt(width)
    gradient_factor = LOGIT_SHARPNESS * scale_factor
    left = images.astype(jnp.bfloat16)
    right = texts.astype(jnp.bfloat16)
    target_signs = (jnp.arange(rows, dtype=jnp.int32)[None, :] == positives[:, None]).astype(
        jnp.float32
    )
    weights, stats = pair_terms(similarity(left, right, scale_factor), target_signs)
    image_acc = row_sum(weights, right)
    text_gradient_total = column_sum(weights, left)
    packed = right[None]
    count = packed.shape[0]
    arrived = []
    for step in range(rounds):
        spread_one = lax.all_to_all(packed, "dp", split_axis=1, concat_axis=1, tiled=True)
        reorder_slots = spread_one.reshape(count, peers, share, width)
        arrived.append(
            lax.all_to_all(
                jnp.take(reorder_slots, plan[step], axis=1).reshape(count, rows, width),
                "dp",
                split_axis=1,
                concat_axis=1,
                tiled=True,
            )
        )
    returned = []
    for step in range(rounds):
        their_right = arrived[step][count - 1]
        forward, extra = pair_terms(similarity(left, their_right, scale_factor), 0.0)
        stats = stats + extra
        image_acc = image_acc + row_sum(forward, their_right)
        returned.append(column_sum(forward, left) * gradient_factor)
    text_grad = text_gradient_total * gradient_factor
    spread_back = lax.all_to_all(jnp.stack(returned), "dp", split_axis=1, concat_axis=1, tiled=True)
    slots = spread_back.reshape(rounds, peers, share, width)
    summed = jnp.take(slots[0], plan[0], axis=0)
    for step in range(1, rounds):
        summed = summed + jnp.take(slots[step], plan[step], axis=0)
    text_grad = text_grad + lax.all_to_all(
        summed.reshape(rows, width), "dp", split_axis=0, concat_axis=0, tiled=True
    )
    pairs = float(rows * rows * (rounds + 1) * peers * lax.axis_size("blk"))
    totals = lax.psum(stats, ("dp", "blk")) / pairs
    return (image_acc * gradient_factor, text_grad, totals)


def solution(mesh):
    placed = (P(("dp", "blk"), None), P(("dp", "blk"), None), P(("dp", "blk")), P())
    return jax.shard_map(
        body,
        mesh=mesh,
        in_specs=placed,
        out_specs=(P(("dp", "blk"), None), P(("dp", "blk"), None), P()),
        check_vma=False,
    )
```

profile of v0, /device:TPU:1, one launch (start us, length us, event | category | flops | bytes accessed | tf_op | source)
XLA Modules:
  0.0 391.3 jit_solution(8783394955422144393)
XLA Ops:
  0.6 1.1 convert_bitcast_fusion
  1.7 0.5 copy.84
  2.2 0.5 broadcast.174
  2.7 2.4 reduce.8
  5.1 0.8 reshape.142
  6.0 17.2 %all-to-all-start = ((bf16[64,2,1152]{2,1,0:T(2,128)(2,1)}), bf16[64,2,1152]{2,1,0:T(2,128)(2,1)S(1)}, u32[]{:S(2)}, u32[]{:S(2)}) async-start(bf16[64,2,1152]{2,1,0:T(2,128)(2,1)} %reshape.142), calls=%async_computation | async-start | bytes 589824 | tf_op jit(solution)/shard_map/all_to_all | solution.py:55
  23.2 20.5 %all-to-all-done = bf16[64,2,1152]{2,1,0:T(2,128)(2,1)S(1)} async-done(((bf16[64,2,1152]{2,1,0:T(2,128)(2,1)}), bf16[64,2,1152]{2,1,0:T(2,128)(2,1)S(1)}, u32[]{:S(2)}, u32[]{:S(2)}) %all-to-all-start) | async-done | bytes 294944 | tf_op jit(solution)/shard_map/all_to_all | solution.py:55
  43.7 0.2 reshape.143
  44.0 1.7 bitcast_reduce_fusion
  45.6 0.1 reshape.114
  45.8 1.2 gather_fusion
  47.0 0.3 broadcast_select_fusion.2
  47.3 0.3 reshape.133
  47.6 2.4 reduce.9
  50.0 0.8 reshape.144
  50.8 7.0 %all-to-all-start.1 = ((bf16[64,2,1152]{2,1,0:T(2,128)(2,1)}), bf16[64,2,1152]{2,1,0:T(2,128)(2,1)S(1)}, u32[]{:S(2)}, u32[]{:S(2)}) async-start(bf16[64,2,1152]{2,1,0:T(2,128)(2,1)} %reshape.144), calls=%async_computation.1 | async-start | bytes 589824 | tf_op jit(solution)/shard_map/all_to_all | solution.py:58
  57.8 1.2 gather_fusion.2
  59.0 1.2 gather_fusion.1
  60.2 0.6 broadcast_select_fusion
  60.9 0.3 reshape.135
  61.1 2.4 reduce.10
  63.6 0.8 reshape.146
  64.4 14.0 %all-to-all-done.1 = bf16[64,2,1152]{2,1,0:T(2,128)(2,1)S(1)} async-done(((bf16[64,2,1152]{2,1,0:T(2,128)(2,1)}), bf16[64,2,1152]{2,1,0:T(2,128)(2,1)S(1)}, u32[]{:S(2)}, u32[]{:S(2)}) %all-to-all-start.1) | async-done | bytes 294944 | tf_op jit(solution)/shard_map/all_to_all | solution.py:58
  78.4 7.0 %all-to-all-start.2 = ((bf16[64,2,1152]{2,1,0:T(2,128)(2,1)}), bf16[64,2,1152]{2,1,0:T(2,128)(2,1)S(1)}, u32[]{:S(2)}, u32[]{:S(2)}) async-start(bf16[64,2,1152]{2,1,0:T(2,128)(2,1)} %reshape.146), calls=%async_computation.2 | async-start | bytes 589824 | tf_op jit(solution)/shard_map/all_to_all | solution.py:58
  85.3 0.3 reshape.137
  85.6 2.4 reduce.11
  88.0 0.8 reshape.148
  88.8 17.0 %all-to-all-done.2 = bf16[64,2,1152]{2,1,0:T(2,128)(2,1)S(1)} async-done(((bf16[64,2,1152]{2,1,0:T(2,128)(2,1)}), bf16[64,2,1152]{2,1,0:T(2,128)(2,1)S(1)}, u32[]{:S(2)}, u32[]{:S(2)}) %all-to-all-start.2) | async-done | bytes 294944 | tf_op jit(solution)/shard_map/all_to_all | solution.py:58
  105.9 7.0 %all-to-all-start.3 = ((bf16[64,2,1152]{2,1,0:T(2,128)(2,1)}), bf16[64,2,1152]{2,1,0:T(2,128)(2,1)S(1)}, u32[]{:S(2)}, u32[]{:S(2)}) async-start(bf16[64,2,1152]{2,1,0:T(2,128)(2,1)} %reshape.148), calls=%async_computation.3 | async-start | bytes 589824 | tf_op jit(solution)/shard_map/all_to_all | solution.py:58
  112.9 0.3 reshape.145
  113.2 0.3 reshape.147
  113.5 1.0 fusion.23
  114.5 0.9 fusion.25
  115.4 18.0 %all-to-all-done.3 = bf16[64,2,1152]{2,1,0:T(2,128)(2,1)S(1)} async-done(((bf16[64,2,1152]{2,1,0:T(2,128)(2,1)}), bf16[64,2,1152]{2,1,0:T(2,128)(2,1)S(1)}, u32[]{:S(2)}, u32[]{:S(2)}) %all-to-all-start.3) | async-done | bytes 294944 | tf_op jit(solution)/shard_map/all_to_all | solution.py:58
  133.4 0.2 reshape.149
  133.7 1.0 fusion.27
  134.7 0.3 fusion.4
  135.0 0.3 fusion.3
  135.3 0.3 fusion.2
  135.6 0.1 pad_maximum_fusion
  135.7 1.2 copy.38
  136.9 115.6 %all_to_all.36 = f32[3,128,1152]{2,0,1:T(4,128)S(1)} all-to-all(f32[3,128,1152]{2,0,1:T(4,128)S(1)} %copy.38), channel_id=1, replica_groups=mesh['dp'=64,'blk'=8] {'dp'}, dimensions={1} | all-to-all | bytes 3538944 | tf_op jit(solution)/shard_map/all_to_all | solution.py:74
  252.4 4.6 %slice_reduce_fusion.2 = (f32[128,1152]{1,0:T(8,128)S(1)}, f32[128,1152]{1,0:T(8,128)S(1)}, f32[128,1152]{1,0:T(8,128)S(1)}) fusion(f32[3,128,1152]{2,0,1:T(4,128)S(1)} %all_to_all.36), kind=kLoop, calls=%fused_computation.21 | loop fusion | bytes 3538944 | tf_op jit(solution)/shard_map/slice | solution.py:76
  257.0 0.3 squeeze.38
  257.4 1.2 gather_fusion.5
  258.6 0.3 squeeze.37
  259.0 1.2 gather_fusion.4
  260.2 0.3 squeeze.36
  260.5 1.2 gather_fusion.3
  261.8 1.5 select_add_fusion
  263.3 7.3 %all-to-all-start.5 = ((f32[64,2,1152]{2,1,0:T(2,128)}), f32[64,2,1152]{2,1,0:T(2,128)S(1)}, u32[]{:S(2)}, u32[]{:S(2)}) async-start(f32[64,2,1152]{2,1,0:T(2,128)} %select_add_fusion), calls=%async_computation.5 | async-start | bytes 1179648 | tf_op jit(solution)/shard_map/all_to_all | solution.py:79
  270.6 0.2 fusion.64
  270.9 0.1 copy.28
  271.0 0.1 copy.29
  271.1 0.8 fusion.21
  271.8 7.6 %fusion.62 = f32[3]{0:T(128)S(1)} fusion(f32[1]{0:T(128)} %bitcast.15, f32[1]{0:T(128)} %bitcast.14, f32[1]{0:T(128)} %bitcast.13, f32[1]{0:T(128)} %bitcast.19, f32[1]{0:T(128)} %bitcast.17, f32[1]{0:T(128)} %bitcast.16, f32[1]{0:T(128)} %bitcast.23, f32[1]{0:T(128)} %bitcast.21, f32[1]{0:T(128)} %bitcast.20, f32[1]{0:T(128)} %bitcast.27, f32[1]{0:T(128)} %bitcast.25, ...), kind=kLoop, calls=%fused_computation.120 | loop fusion | flops 33 | bytes 60 | tf_op jit(solution)/shard_map/add | solution.py:70
  279.5 0.3 fusion.59
  279.8 107.9 %psum.7 = f32[3]{0:T(128)S(1)} all-reduce(f32[3]{0:T(128)S(1)} %fusion.62), channel_id=1, replica_groups=mesh['dp'=64,'blk'=8] {'dp','blk'}, use_global_device_ids=true, to_apply=%region_12.15 | all-reduce | flops 3 | bytes 24 | tf_op jit(solution)/shard_map/psum | solution.py:83
  387.7 0.5 broadcast_multiply_fusion.1
  388.2 0.2 convolution_add_fusion.2
  388.4 0.2 convolution_add_fusion.1
  388.7 1.1 fusion.1
  389.7 0.4 all_to_all.29
  390.2 1.1 fusion
  (27 shorter events, 0.1 us)
Async XLA Ops:
  0.6 22.6 %copy-start.9 = (s32[3,64]{1,0:T(4,128)S(1)}, s32[3,64]{1,0:T(4,128)}, u32[]{:S(2)}) copy-start(s32[3,64]{1,0:T(4,128)} %param.11) | copy-start | bytes 2308
  6.0 37.8 %all-to-all-start = ((bf16[64,2,1152]{2,1,0:T(2,128)(2,1)}), bf16[64,2,1152]{2,1,0:T(2,128)(2,1)S(1)}, u32[]{:S(2)}, u32[]{:S(2)}) async-start(bf16[64,2,1152]{2,1,0:T(2,128)(2,1)} %reshape.142), calls=%async_computation | async-start | bytes 589824 | tf_op jit(solution)/shard_map/all_to_all | solution.py:55
  50.8 27.5 %all-to-all-start.1 = ((bf16[64,2,1152]{2,1,0:T(2,128)(2,1)}), bf16[64,2,1152]{2,1,0:T(2,128)(2,1)S(1)}, u32[]{:S(2)}, u32[]{:S(2)}) async-start(bf16[64,2,1152]{2,1,0:T(2,128)(2,1)} %reshape.144), calls=%async_computation.1 | async-start | bytes 589824 | tf_op jit(solution)/shard_map/all_to_all | solution.py:58
  64.4 48.5 %copy-start.7 = (f32[128,1152]{1,0:T(8,128)S(1)}, f32[128,1152]{1,0:T(8,128)}, u32[]{:S(2)}) copy-start(f32[128,1152]{1,0:T(8,128)} %param.8) | copy-start | bytes 1769476
  78.4 27.5 %all-to-all-start.2 = ((bf16[64,2,1152]{2,1,0:T(2,128)(2,1)}), bf16[64,2,1152]{2,1,0:T(2,128)(2,1)S(1)}, u32[]{:S(2)}, u32[]{:S(2)}) async-start(bf16[64,2,1152]{2,1,0:T(2,128)(2,1)} %reshape.146), calls=%async_computation.2 | async-start | bytes 589824 | tf_op jit(solution)/shard_map/all_to_all | solution.py:58
  105.9 27.5 %all-to-all-start.3 = ((bf16[64,2,1152]{2,1,0:T(2,128)(2,1)}), bf16[64,2,1152]{2,1,0:T(2,128)(2,1)S(1)}, u32[]{:S(2)}, u32[]{:S(2)}) async-start(bf16[64,2,1152]{2,1,0:T(2,128)(2,1)} %reshape.148), calls=%async_computation.3 | async-start | bytes 589824 | tf_op jit(solution)/shard_map/all_to_all | solution.py:58
  113.2 20.5 %copy-start.3 = (bf16[128,1,1152]{2,1,0:T(2,128)(2,1)}, bf16[128,1,1152]{2,1,0:T(2,128)(2,1)S(1)}, u32[]{:S(2)}) copy-start(bf16[128,1,1152]{2,1,0:T(2,128)(2,1)S(1)} %reshape.145) | copy-start | bytes 884740
  113.5 21.2 %copy-start.1 = (bf16[128,1,1152]{2,1,0:T(2,128)(2,1)}, bf16[128,1,1152]{2,1,0:T(2,128)(2,1)S(1)}, u32[]{:S(2)}) copy-start(bf16[128,1,1152]{2,1,0:T(2,128)(2,1)S(1)} %reshape.147) | copy-start | bytes 884740
  133.7 1.9 copy-start.5
  261.8 8.9 %copy-start = (f32[128,1152]{1,0:T(8,128)S(1)}, f32[128,1152]{1,0:T(8,128)}, u32[]{:S(2)}) copy-start(f32[128,1152]{1,0:T(8,128)} %param.9) | copy-start | bytes 1769476
  263.2 7.8 %copy-start.8 = (s32[128]{0:T(128)S(1)}, s32[128]{0:T(128)}, u32[]{:S(2)}) copy-start(s32[128]{0:T(128)} %param.10) | copy-start | bytes 1540
  263.2 124.9 %copy-start.4 = (bf16[128,1,1152]{2,1,0:T(2,128)(2,1)S(1)}, bf16[128,1,1152]{2,1,0:T(2,128)(2,1)}, u32[]{:S(2)}) copy-start(bf16[128,1,1152]{2,1,0:T(2,128)(2,1)} %copy-done.3) | copy-start | bytes 884740
  263.3 126.5 %all-to-all-start.5 = ((f32[64,2,1152]{2,1,0:T(2,128)}), f32[64,2,1152]{2,1,0:T(2,128)S(1)}, u32[]{:S(2)}, u32[]{:S(2)}) async-start(f32[64,2,1152]{2,1,0:T(2,128)} %select_add_fusion), calls=%async_computation.5 | async-start | bytes 1179648 | tf_op jit(solution)/shard_map/all_to_all | solution.py:79
  270.9 117.6 %copy-start.2 = (bf16[128,1,1152]{2,1,0:T(2,128)(2,1)S(1)}, bf16[128,1,1152]{2,1,0:T(2,128)(2,1)}, u32[]{:S(2)}) copy-start(bf16[128,1,1152]{2,1,0:T(2,128)(2,1)} %copy-done.1) | copy-start | bytes 884740
  279.8 108.9 %copy-start.6 = (bf16[128,1,1152]{2,1,0:T(2,128)(2,1)S(1)}, bf16[128,1,1152]{2,1,0:T(2,128)(2,1)}, u32[]{:S(2)}) copy-start(bf16[128,1,1152]{2,1,0:T(2,128)(2,1)} %copy-done.5) | copy-start | bytes 884740
where the time goes:
time: 392 us; the launch traced here: 391 us
  blocking collectives  223 us (57%)
  waiting for transfers between devices  69.5 us (18%)
  starting transfers between devices  45.5 us (12%)
  local copies, waits for them, and re-layouts  22.5 us (6%)
  other arithmetic  22.3 us (6%)
  matrix products  6.93 us (2%)
    all_to_all x1, blocking collectives, body(): lax.all_to_all(jnp.stack(returned), 'dp', split_axis=1, concat_axis=1, ti...  116 us
    psum x1, blocking collectives, body(): totals = lax.psum(stats, ('dp', 'blk')) / pairs  108 us
    all_to_all x3, waiting for transfers between devices, body(): lax.all_to_all(jnp.take(reorder_slots, plan[step], axis=1).reshape(count,...  49 us
    all_to_all x3, starting transfers between devices, body(): lax.all_to_all(jnp.take(reorder_slots, plan[step], axis=1).reshape(count,...  20.9 us
    all_to_all x1, waiting for transfers between devices, body(): lax.all_to_all(packed, 'dp', split_axis=1, concat_axis=1, tiled=True)  20.5 us
    all_to_all x1, starting transfers between devices, body(): lax.all_to_all(packed, 'dp', split_axis=1, concat_axis=1, tiled=True)  17.2 us
    unnamed x4, other arithmetic  9.59 us
  transfers between devices with their start and end apart: 5, of which 4 were waited for; matrix products, arithmetic and copies ran while one was open for 6% of the time, Pallas kernels for 0%

commit v1 on v0

--- a/solution.py
+++ b/solution.py
@@ -71,7 +71,12 @@
         image_acc = image_acc + row_sum(forward, their_right)
         returned.append(column_sum(forward, left) * gradient_factor)
     text_grad = text_gradient_total * gradient_factor
-    spread_back = lax.all_to_all(jnp.stack(returned), "dp", split_axis=1, concat_axis=1, tiled=True)
+    spread_back = jnp.concatenate(
+        lax.all_to_all(
+            jnp.stack(jnp.split(jnp.stack(returned), lax.axis_size("dp"), axis=1)), "dp", 0, 0
+        ),
+        axis=1,
+    )
     slots = spread_back.reshape(rounds, peers, share, width)
     summed = jnp.take(slots[0], plan[0], axis=0)
     for step in range(1, rounds):

time: 392 us -> 364 us (0.929)
  blocking collectives: 223 us -> 197 us
  local copies, waits for them, and re-layouts: 22.5 us -> 17.6 us
    all_to_all x1, blocking collectives: 116 us -> 88.7 us  [body(): lax.all_to_all(jnp.stack(jnp.split(jnp.stack(returned), lax.axis_size('dp...]
    slice x1 -> x0, local copies, waits for them, and re-layouts: 4.57 us -> none  [body(): summed = jnp.take(slots[0], plan[0], axis=0)]
  transfers between devices with their start and end apart: 5 -> 5, of which waited for: 4 -> 4; matrix products, arithmetic and copies ran while one was open for 6% -> 7% of each run, Pallas kernels for 0% -> 0%
where the time goes in v1:
time: 364 us; the launch traced here: 363 us
  blocking collectives  197 us (54%)
  waiting for transfers between devices  70.4 us (19%)
  starting transfers between devices  46.7 us (13%)
  other arithmetic  22.2 us (6%)
  local copies, waits for them, and re-layouts  17.6 us (5%)
  matrix products  7.99 us (2%)
    psum x1, blocking collectives, body(): totals = lax.psum(stats, ('dp', 'blk')) / pairs  108 us
    all_to_all x1, blocking collectives, body(): lax.all_to_all(jnp.stack(jnp.split(jnp.stack(returned), lax.axis_size('dp...  88.7 us
    all_to_all x3, waiting for transfers between devices, body(): lax.all_to_all(jnp.take(reorder_slots, plan[step], axis=1).reshape(count,...  49.9 us
    all_to_all x3, starting transfers between devices, body(): lax.all_to_all(jnp.take(reorder_slots, plan[step], axis=1).reshape(count,...  20.9 us
    all_to_all x1, waiting for transfers between devices, body(): lax.all_to_all(packed, 'dp', split_axis=1, concat_axis=1, tiled=True)  20.5 us
    all_to_all x1, starting transfers between devices, body(): lax.all_to_all(packed, 'dp', split_axis=1, concat_axis=1, tiled=True)  17.2 us
    unnamed x4, other arithmetic  9.59 us
    all_to_all x1, starting transfers between devices, body(): lax.all_to_all(summed.reshape(rows, width), 'dp', split_axis=0, concat_ax...  8.55 us
  transfers between devices with their start and end apart: 5, of which 4 were waited for; matrix products, arithmetic and copies ran while one was open for 7% of the time, Pallas kernels for 0%

profile of v1, /device:TPU:1, one launch (start us, length us, event | category | flops | bytes accessed | tf_op | source)
XLA Modules:
  0.0 362.9 jit_solution(331304443327796826)
XLA Ops:
  0.6 1.1 convert_bitcast_fusion
  1.7 0.5 copy.79
  2.2 0.5 broadcast.171
  2.7 2.4 reduce.2
  5.1 0.8 reshape.136
  6.0 17.2 %all-to-all-start = ((bf16[64,2,1152]{2,1,0:T(2,128)(2,1)}), bf16[64,2,1152]{2,1,0:T(2,128)(2,1)S(1)}, u32[]{:S(2)}, u32[]{:S(2)}) async-start(bf16[64,2,1152]{2,1,0:T(2,128)(2,1)} %reshape.136), calls=%async_computation | async-start | bytes 589824 | tf_op jit(solution)/shard_map/all_to_all | solution.py:55
  23.2 20.5 %all-to-all-done = bf16[64,2,1152]{2,1,0:T(2,128)(2,1)S(1)} async-done(((bf16[64,2,1152]{2,1,0:T(2,128)(2,1)}), bf16[64,2,1152]{2,1,0:T(2,128)(2,1)S(1)}, u32[]{:S(2)}, u32[]{:S(2)}) %all-to-all-start) | async-done | bytes 294944 | tf_op jit(solution)/shard_map/all_to_all | solution.py:55
  43.7 0.2 reshape.137
  44.0 1.7 bitcast_reduce_fusion
  45.6 0.1 reshape.111
  45.8 1.2 gather_fusion.2
  47.0 1.2 gather_fusion.1
  48.2 0.6 broadcast_select_fusion
  48.8 0.3 reshape.134
  49.1 2.4 reduce.5
  51.5 0.8 reshape.142
  52.3 7.0 %all-to-all-start.3 = ((bf16[64,2,1152]{2,1,0:T(2,128)(2,1)}), bf16[64,2,1152]{2,1,0:T(2,128)(2,1)S(1)}, u32[]{:S(2)}, u32[]{:S(2)}) async-start(bf16[64,2,1152]{2,1,0:T(2,128)(2,1)} %reshape.142), calls=%async_computation.3 | async-start | bytes 589824 | tf_op jit(solution)/shard_map/all_to_all | solution.py:58
  59.3 1.2 gather_fusion
  60.5 0.3 broadcast_select_fusion.2
  60.9 0.3 reshape.130
  61.1 2.4 reduce.3
  63.5 0.8 reshape.138
  64.4 15.5 %all-to-all-done.3 = bf16[64,2,1152]{2,1,0:T(2,128)(2,1)S(1)} async-done(((bf16[64,2,1152]{2,1,0:T(2,128)(2,1)}), bf16[64,2,1152]{2,1,0:T(2,128)(2,1)S(1)}, u32[]{:S(2)}, u32[]{:S(2)}) %all-to-all-start.3) | async-done | bytes 294944 | tf_op jit(solution)/shard_map/all_to_all | solution.py:58
  79.8 7.0 %all-to-all-start.1 = ((bf16[64,2,1152]{2,1,0:T(2,128)(2,1)}), bf16[64,2,1152]{2,1,0:T(2,128)(2,1)S(1)}, u32[]{:S(2)}, u32[]{:S(2)}) async-start(bf16[64,2,1152]{2,1,0:T(2,128)(2,1)} %reshape.138), calls=%async_computation.1 | async-start | bytes 589824 | tf_op jit(solution)/shard_map/all_to_all | solution.py:58
  86.8 0.3 reshape.132
  87.1 2.4 reduce.4
  89.5 0.8 reshape.140
  90.3 17.0 %all-to-all-done.1 = bf16[64,2,1152]{2,1,0:T(2,128)(2,1)S(1)} async-done(((bf16[64,2,1152]{2,1,0:T(2,128)(2,1)}), bf16[64,2,1152]{2,1,0:T(2,128)(2,1)S(1)}, u32[]{:S(2)}, u32[]{:S(2)}) %all-to-all-start.1) | async-done | bytes 294944 | tf_op jit(solution)/shard_map/all_to_all | solution.py:58
  107.4 7.0 %all-to-all-start.2 = ((bf16[64,2,1152]{2,1,0:T(2,128)(2,1)}), bf16[64,2,1152]{2,1,0:T(2,128)(2,1)S(1)}, u32[]{:S(2)}, u32[]{:S(2)}) async-start(bf16[64,2,1152]{2,1,0:T(2,128)(2,1)} %reshape.140), calls=%async_computation.2 | async-start | bytes 589824 | tf_op jit(solution)/shard_map/all_to_all | solution.py:58
  114.4 0.3 reshape.143
  114.7 0.3 reshape.139
  115.0 0.0 copy-start.1
  115.0 1.0 fusion.23
  115.9 0.3 fusion.2
  116.2 1.0 fusion.27
  117.2 0.3 fusion.4
  117.5 17.4 %all-to-all-done.2 = bf16[64,2,1152]{2,1,0:T(2,128)(2,1)S(1)} async-done(((bf16[64,2,1152]{2,1,0:T(2,128)(2,1)}), bf16[64,2,1152]{2,1,0:T(2,128)(2,1)S(1)}, u32[]{:S(2)}, u32[]{:S(2)}) %all-to-all-start.2) | async-done | bytes 294944 | tf_op jit(solution)/shard_map/all_to_all | solution.py:58
  134.9 0.2 reshape.141
  135.2 0.0 copy-start.3
  135.2 1.0 fusion.25
  136.1 0.3 fusion.3
  136.4 0.2 pad_maximum_fusion
  138.2 88.7 %all_to_all.36 = f32[64,3,2,1152]{3,2,1,0:T(2,128)S(1)} all-to-all(f32[64,3,2,1152]{3,2,1,0:T(2,128)S(1)} %constant_dynamic-update-slice_fusion), channel_id=1, replica_groups=mesh['dp'=64,'blk'=8] {'dp'}, dimensions={0} | all-to-all | bytes 3538944 | tf_op jit(solution)/shard_map/all_to_all | solution.py:75
  226.9 0.6 slice_bitcast_fusion.2
  227.5 1.2 gather_fusion.3
  228.7 1.2 gather_fusion.5
  229.9 1.2 gather_fusion.4
  231.2 0.0 copy-start
  231.2 1.5 select_add_fusion
  232.7 8.6 %all-to-all-start.5 = ((f32[64,2,1152]{2,1,0:T(2,128)}), f32[64,2,1152]{2,1,0:T(2,128)S(1)}, u32[]{:S(2)}, u32[]{:S(2)}) async-start(f32[64,2,1152]{2,1,0:T(2,128)} %select_add_fusion), calls=%async_computation.5 | async-start | bytes 1179648 | tf_op jit(solution)/shard_map/all_to_all | solution.py:84
  241.2 0.2 fusion.64
  241.5 0.1 copy.27
  241.6 0.1 copy.28
  241.7 0.8 fusion.21
  242.5 7.6 %fusion.62 = f32[3]{0:T(128)S(1)} fusion(f32[1]{0:T(128)} %bitcast.83, f32[1]{0:T(128)} %bitcast.82, f32[1]{0:T(128)} %bitcast.81, f32[1]{0:T(128)} %bitcast.87, f32[1]{0:T(128)} %bitcast.85, f32[1]{0:T(128)} %bitcast.84, f32[1]{0:T(128)} %bitcast.91, f32[1]{0:T(128)} %bitcast.89, f32[1]{0:T(128)} %bitcast.88, f32[1]{0:T(128)} %bitcast.95, f32[1]{0:T(128)} %bitcast.93, ...), kind=kLoop, calls=%fused_computation.248 | loop fusion | flops 33 | bytes 60 | tf_op jit(solution)/shard_map/add | solution.py:70
  250.0 0.3 fusion.59
  250.3 107.9 %psum.7 = f32[3]{0:T(128)S(1)} all-reduce(f32[3]{0:T(128)S(1)} %fusion.62), channel_id=1, replica_groups=mesh['dp'=64,'blk'=8] {'dp','blk'}, use_global_device_ids=true, to_apply=%region_12.15 | all-reduce | flops 3 | bytes 24 | tf_op jit(solution)/shard_map/psum | solution.py:88
  358.2 0.5 broadcast_multiply_fusion.1
  358.7 0.2 convolution_add_fusion.2
  358.9 1.3 convolution_add_fusion.1
  360.2 1.1 fusion.1
  361.3 0.0 all-to-all-done.5
  361.3 0.4 all_to_all.29
  361.7 1.2 fusion
  (81 shorter events, 1.4 us)
Async XLA Ops:
  0.6 22.6 %copy-start.6 = (s32[3,64]{1,0:T(4,128)S(1)}, s32[3,64]{1,0:T(4,128)}, u32[]{:S(2)}) copy-start(s32[3,64]{1,0:T(4,128)} %param.11) | copy-start | bytes 2308
  6.0 37.8 %all-to-all-start = ((bf16[64,2,1152]{2,1,0:T(2,128)(2,1)}), bf16[64,2,1152]{2,1,0:T(2,128)(2,1)S(1)}, u32[]{:S(2)}, u32[]{:S(2)}) async-start(bf16[64,2,1152]{2,1,0:T(2,128)(2,1)} %reshape.136), calls=%async_computation | async-start | bytes 589824 | tf_op jit(solution)/shard_map/all_to_all | solution.py:55
  52.3 27.5 %all-to-all-start.3 = ((bf16[64,2,1152]{2,1,0:T(2,128)(2,1)}), bf16[64,2,1152]{2,1,0:T(2,128)(2,1)S(1)}, u32[]{:S(2)}, u32[]{:S(2)}) async-start(bf16[64,2,1152]{2,1,0:T(2,128)(2,1)} %reshape.142), calls=%async_computation.3 | async-start | bytes 589824 | tf_op jit(solution)/shard_map/all_to_all | solution.py:58
  64.4 50.0 %copy-start.4 = (f32[128,1152]{1,0:T(8,128)S(1)}, f32[128,1152]{1,0:T(8,128)}, u32[]{:S(2)}) copy-start(f32[128,1152]{1,0:T(8,128)} %param.8) | copy-start | bytes 1769476
  79.8 27.5 %all-to-all-start.1 = ((bf16[64,2,1152]{2,1,0:T(2,128)(2,1)}), bf16[64,2,1152]{2,1,0:T(2,128)(2,1)S(1)}, u32[]{:S(2)}, u32[]{:S(2)}) async-start(bf16[64,2,1152]{2,1,0:T(2,128)(2,1)} %reshape.138), calls=%async_computation.1 | async-start | bytes 589824 | tf_op jit(solution)/shard_map/all_to_all | solution.py:58
  107.4 27.5 %all-to-all-start.2 = ((bf16[64,2,1152]{2,1,0:T(2,128)(2,1)}), bf16[64,2,1152]{2,1,0:T(2,128)(2,1)S(1)}, u32[]{:S(2)}, u32[]{:S(2)}) async-start(bf16[64,2,1152]{2,1,0:T(2,128)(2,1)} %reshape.140), calls=%async_computation.2 | async-start | bytes 589824 | tf_op jit(solution)/shard_map/all_to_all | solution.py:58
  115.0 1.0 copy-start.1
  135.2 91.7 %copy-start.3 = (bf16[128,1,1152]{2,1,0:T(2,128)(2,1)}, bf16[128,1,1152]{2,1,0:T(2,128)(2,1)S(1)}, u32[]{:S(2)}) copy-start(bf16[128,1,1152]{2,1,0:T(2,128)(2,1)S(1)} %reshape.141) | copy-start | bytes 884740
  231.2 10.1 %copy-start = (f32[128,1152]{1,0:T(8,128)S(1)}, f32[128,1152]{1,0:T(8,128)}, u32[]{:S(2)}) copy-start(f32[128,1152]{1,0:T(8,128)} %param.9) | copy-start | bytes 1769476
  232.7 9.0 %copy-start.5 = (s32[128]{0:T(128)S(1)}, s32[128]{0:T(128)}, u32[]{:S(2)}) copy-start(s32[128]{0:T(128)} %param.10) | copy-start | bytes 1540
  232.7 126.0 %copy-start.2 = (bf16[128,1,1152]{2,1,0:T(2,128)(2,1)S(1)}, bf16[128,1,1152]{2,1,0:T(2,128)(2,1)}, u32[]{:S(2)}) copy-start(bf16[128,1,1152]{2,1,0:T(2,128)(2,1)} %copy-done.1) | copy-start | bytes 884740
  232.7 128.6 %all-to-all-start.5 = ((f32[64,2,1152]{2,1,0:T(2,128)}), f32[64,2,1152]{2,1,0:T(2,128)S(1)}, u32[]{:S(2)}, u32[]{:S(2)}) async-start(f32[64,2,1152]{2,1,0:T(2,128)} %select_add_fusion), calls=%async_computation.5 | async-start | bytes 1179648 | tf_op jit(solution)/shard_map/all_to_all | solution.py:84
